TPU v7x, 32 devices: a whole 2x2x4 slice. The times are simulated.
32 devices in a mesh: tm: 8 (over y, x, core), head: 4 (over z).
Axes of the slice: x: 2, y: 2, z: 4, core: 2. Of those that a mesh axis runs over, the one named last changes fastest.
Arguments:
- query_rows: bfloat16 [2048, 4096], P('tm', 'head'), may hold values from -6 to 6
- key_rows: bfloat16 [2048, 4096], P('tm', 'head'), may hold values from -6 to 6
- value_rows: bfloat16 [2048, 4096], P('tm', 'head'), may hold values from -12 to 12
- frame_counts: int32 [8], replicated, may hold values from 1 to 4, 24 in all
- history: bfloat16 [16, 4096], P('tm', 'head'), may hold values from -3 to 3
- offsets: int32 [8, 8], P('tm'), may hold values from 0 to 7, each once within a row
- cotangent: bfloat16 [2176, 2048], P('tm'), may hold values from -0.1875 to 0.1875
Outputs:
- attended: bfloat16 [2048, 4096], P('tm', 'head')
- disc_grad: float32 [2048, 4096], P('tm', 'head')
Inputs may be any that keep to these rules, and one draw needn't show every extreme that they name: Each row of offsets names every number below 8 once.
All inputs are finite; a program needn't handle non-finite values.
Results may differ from a plain program's by a relative error of at most 0.0049.
Values may be sent and summed in bfloat16 or wider, within the bound.
No kernel may reach another device: no remote copies, remote signals or barrier semaphores. Data moves between devices by JAX's collectives and lax.ppermute only.
A program may use at most 64 MiB of HBM per device.

v0:
```python
import math

import jax
import jax.numpy as jnp
from jax import lax
from jax.sharding import PartitionSpec as P

HD = 128
TPF = 64
WINB = 4


def from_behind(x, axis, by):
    devices = lax.axis_size(axis)
    pairs = [(i, i + by) for i in range(devices) if 0 <= i + by < devices]
    return lax.ppermute(x, axis, pairs)


def body(query_rows, key_rows, value_rows, frame_counts, history, offsets, cotangent):
    tok_rows, feat_width = query_rows.shape
    local_heads = feat_width // HD
    block_total = lax.axis_size("tm")
    own_block = lax.axis_index("tm")
    score_scale = 1.0 / math.sqrt(HD)
    key_value = jnp.stack([key_rows, value_rows])
    pieces = []
    for distance in range(WINB - 1, 0, -1):
        pieces.append(from_behind(key_value, "tm", distance))
    window = jnp.concatenate(pieces + [key_value], axis=1)
    source_block = own_block - (WINB - 1) + jnp.arange(WINB, dtype=jnp.int32)
    block_match = jnp.arange(block_total, dtype=jnp.int32)[None, :] == source_block[:, None]
    block_count = jnp.sum(jnp.where(block_match, frame_counts[None, :], 0), axis=1)
    frame_index = jnp.arange(tok_rows, dtype=jnp.int32) // TPF
    kept_mask = (
        (source_block[:, None] >= 0) & (frame_index[None, :] < block_count[:, None])
    ).reshape(WINB * tok_rows)
    key_window = window[0].reshape(WINB * tok_rows, local_heads, HD)
    value_window = window[1].reshape(WINB * tok_rows, local_heads, HD)
    query_heads = query_rows.reshape(tok_rows, local_heads, HD)
    scores = (
        jnp.einsum("qhd,khd->hqk", query_heads, key_window, preferred_element_type=jnp.float32)
        * score_scale
    )
    scores = jnp.where(kept_mask[None, None, :], scores, -jnp.inf)
    row_max = jnp.max(scores, axis=-1, keepdims=True)
    weights = jnp.exp(scores - row_max)
    probs = (weights / jnp.sum(weights, axis=-1, keepdims=True)).astype(jnp.bfloat16)
    mixed = jnp.einsum("hqk,khd->qhd", probs, value_window, preferred_element_type=jnp.float32)
    attended = mixed.astype(jnp.bfloat16).reshape(tok_rows, feat_width)
    tile_rows = history.shape[0]
    source_tile = (own_block - offsets[0]) % block_total
    source_row = (
        source_tile[:, None] * tile_rows + jnp.arange(tile_rows, dtype=jnp.int32)[None, :]
    ).reshape(-1)
    incoming = lax.all_gather(history, "tm", axis=0, tiled=True)
    piece_rows = incoming.shape[0]
    selector = (source_row[:, None] == jnp.arange(piece_rows, dtype=jnp.int32)[None, :]).astype(
        jnp.bfloat16
    )
    clip_hist = jnp.dot(selector, incoming, preferred_element_type=jnp.float32).astype(jnp.bfloat16)
    disc_clip = jnp.concatenate([clip_hist, attended], axis=0)
    disc_grad = lax.psum_scatter(
        lax.dot_general(
            cotangent, disc_clip, (((0,), (0,)), ((), ())), preferred_element_type=jnp.float32
        ),
        "tm",
        scatter_dimension=0,
        tiled=True,
    )
    return (attended, disc_grad)


def solution(mesh):
    in_specs = (
        P("tm", "head"),
        P("tm", "head"),
        P("tm", "head"),
        P(),
        P("tm", "head"),
        P("tm", None),
        P("tm", None),
    )
    out_specs = (P("tm", "head"), P("tm", "head"))
    return jax.shard_map(body, mesh=mesh, in_specs=in_specs, out_specs=out_specs, check_vma=False)
```

profile of v0, /device:TPU:0, one launch (start us, length us, event | category | flops | bytes accessed | tf_op | source)
XLA Modules:
  0.0 180.0 jit_solution(6165414970335479926)
XLA Ops:
  7.2 0.0 copy-start
  7.2 0.0 copy-start.2
  7.2 0.0 copy-start.1
  7.2 0.0 copy-start.3
  7.2 0.0 reduce-scatter.2.cloned.1.call-start
  7.3 1.3 copy.30
  8.6 1.2 copy.29
  9.8 0.1 pad_maximum_fusion
  9.9 3.4 %collective-permute-start.2 = (bf16[2,256,1024]{1,2,0:T(8,128)(2,1)S(1)}, bf16[2,256,1024]{1,2,0:T(8,128)(2,1)}, u32[]{:S(2)}, u32[]{:S(2)}) collective-permute-start(bf16[2,256,1024]{1,2,0:T(8,128)(2,1)S(1)} %pad_maximum_fusion), channel_id=1, source_target_pairs={{0,4},{4,8},{8,12},{12,16},{16,20},{20,24},{24,28},{1,5},{5,9},{9,... | collective-permute-start | bytes 3145736 | tf_op jit(solution)/shard_map/ppermute | solution.py:16
  13.3 4.5 %collective-permute-start.1 = (bf16[2,256,1024]{1,2,0:T(8,128)(2,1)S(1)}, bf16[2,256,1024]{1,2,0:T(8,128)(2,1)}, u32[]{:S(2)}, u32[]{:S(2)}) collective-permute-start(bf16[2,256,1024]{1,2,0:T(8,128)(2,1)S(1)} %pad_maximum_fusion), channel_id=1, source_target_pairs={{0,8},{4,12},{8,16},{12,20},{16,24},{20,28},{1,9},{5,13},{9,17},{1... | collective-permute-start | bytes 3145736 | tf_op jit(solution)/shard_map/ppermute | solution.py:16
  17.7 4.3 %collective-permute-start = (bf16[2,256,1024]{1,2,0:T(8,128)(2,1)S(1)}, bf16[2,256,1024]{1,2,0:T(8,128)(2,1)}, u32[]{:S(2)}, u32[]{:S(2)}) collective-permute-start(bf16[2,256,1024]{1,2,0:T(8,128)(2,1)S(1)} %pad_maximum_fusion), channel_id=1, source_target_pairs={{0,12},{4,16},{8,20},{12,24},{16,28},{1,13},{5,17},{9,21},{13,25},... | collective-permute-start | bytes 3145736 | tf_op jit(solution)/shard_map/ppermute | solution.py:16
  22.1 0.0 copy-done.2
  22.1 0.2 select_reduce_fusion
  22.3 0.1 compare_and_fusion
  22.3 0.0 copy-done.1
  22.3 53.3 %all-gather = bf16[8,2,1024]{2,1,0:T(2,128)(2,1)S(1)} all-gather(bf16[1,2,1024]{2,1,0:T(2,128)(2,1)S(1)} %bitcast.57), channel_id=1, replica_groups=mesh['tm'=8,'head'=4] {'tm'}, dimensions={0}, use_global_device_ids=true | all-gather | bytes 36864 | tf_op jit(solution)/shard_map/all_gather | solution.py:55
  75.7 0.1 iota_add_fusion
  75.8 0.1 add.57
  75.9 0.2 convolution_convert_fusion
  76.1 0.2 copy.34
  76.3 0.0 collective-permute-done.2
  76.3 0.0 collective-permute-done.1
  76.3 0.0 collective-permute-done
  76.3 2.2 %maximum_maximum_fusion = bf16[2,1024,1024]{1,2,0:T(8,128)(2,1)S(1)} fusion(bf16[1,256,1024]{1,2,0:T(8,128)(2,1)S(1)} %bitcast.50, bf16[1,256,1024]{1,2,0:T(8,128)(2,1)S(1)} %bitcast.52, bf16[2,256,1024]{1,2,0:T(8,128)(2,1)} %collective-permute-done.2, bf16[2,256,1024]{1,2,0:T(8,128)(2,1)} %collective-permute-done.1, ...), kind=kLoop, calls=%fused_computation.8 | loop fusion | flops 20971520 | bytes 8388608 | tf_op jit(solution)/shard_map/concatenate | solution.py:29
  78.5 1.8 %fusion.32 = (bf16[1,1024,1024]{1,2,0:T(8,128)(2,1)S(1)}, bf16[1,1024,1024]{1,2,0:T(8,128)(2,1)}) fusion(bf16[2,1024,1024]{1,2,0:T(8,128)(2,1)S(1)} %maximum_maximum_fusion), kind=kLoop, calls=%fused_computation.45 | loop fusion | bytes 8388608 | tf_op jit(solution)/shard_map/slice | solution.py:37
  80.3 7.2 %fusion.33 = (f32[8,256]{1,0:T(8,128)S(1)}, f32[8,256,1024]{1,2,0:T(8,128)}) fusion(pred[1024]{0:T(1024)(128)(4,1)S(1)} %and.44, bf16[1024,8,128]{0,2,1:T(8,128)(2,1)S(1)} %bitcast.56, bf16[256,1024]{1,0:T(8,128)(2,1)} %param.7), kind=kOutput, calls=%fused_computation.46 | convolution fusion | flops 545260544 | bytes 11019264 | tf_op jit(solution)/shard_map/sub | solution.py:46
  87.5 4.8 %fusion.9 = bf16[8,128,256]{2,1,0:T(8,128)(2,1)S(1)} fusion(bf16[1024,8,128]{0,2,1:T(8,128)(2,1)} %bitcast.55, f32[8,256,1024]{1,2,0:T(8,128)} %get-tuple-element.13, f32[8,256]{1,0:T(8,128)S(1)} %get-tuple-element.12), kind=kOutput, calls=%fused_computation.13 | convolution fusion | flops 541327360 | bytes 11018240 | tf_op jit(solution)/shard_map/hqk,khd->qhd/dot_general | solution.py:48
  92.4 5.6 %convolution_bitcast_fusion = f32[2048,1024]{0,1:T(8,128)} fusion(bf16[272,2048]{1,0:T(8,128)(2,1)S(1)} %copy-done, bf16[256,1024]{0,1:T(8,128)(2,1)S(1)} %bitcast.53, bf16[16,1024]{0,1:T(8,128)(2,1)S(1)} %copy.34), kind=kOutput, calls=%fused_computation.7 | convolution fusion | flops 1141964800 | bytes 10059776 | tf_op jit(solution)/shard_map/dot_general | solution.py:63
  98.0 0.0 reduce-scatter.2.cloned.1.call-update
  98.0 1.0 copy.35
  99.0 71.6 %reduce-scatter.2.cloned.1.call-done = f32[256,1024]{0,1:T(8,128)} async-done(((f32[2048,1024]{0,1:T(8,128)}), f32[256,1024]{0,1:T(8,128)}) %reduce-scatter.2.cloned.1.call-update) | async-done | bytes 1048592 | tf_op jit(solution)/shard_map/reduce_scatter | solution.py:62
  170.7 2.5 %copy.36 = f32[256,1024]{1,0:T(8,128)} copy(f32[256,1024]{0,1:T(8,128)} %reduce-scatter.2.cloned.1.call-done) | data formatting | bytes 2097152
  (8 shorter events, 0.1 us)
Async XLA Ops:
  7.2 85.2 %copy-start = (bf16[272,2048]{1,0:T(8,128)(2,1)S(1)}, bf16[272,2048]{1,0:T(8,128)(2,1)}, u32[]{:S(2)}) copy-start(bf16[272,2048]{1,0:T(8,128)(2,1)} %param.13) | copy-start | bytes 3342340
  7.2 14.9 %copy-start.2 = (s32[8]{0:T(128)S(1)}, s32[8]{0:T(128)}, u32[]{:S(2)}) copy-start(s32[8]{0:T(128)} %param.10) | copy-start | bytes 100
  7.2 15.2 %copy-start.1 = (bf16[2,1024]{1,0:T(2,128)(2,1)S(1)}, bf16[2,1024]{1,0:T(2,128)(2,1)}, u32[]{:S(2)}) copy-start(bf16[2,1024]{1,0:T(2,128)(2,1)} %param.11) | copy-start | bytes 12292
  7.2 68.5 %copy-start.3 = (s32[1,8]{1,0:T(1,128)S(1)}, s32[1,8]{1,0:T(1,128)}, u32[]{:S(2)}) copy-start(s32[1,8]{1,0:T(1,128)} %param.12) | copy-start | bytes 100
  7.2 163.4 %reduce-scatter.2.cloned.1.call-start = ((), (), s32[]{:S(2)}) async-start(), calls=%async_computation.1 | async-start | bytes 9437184 | tf_op jit(solution)/shard_map/reduce_scatter | solution.py:62
  9.9 66.3 %collective-permute-start.2 = (bf16[2,256,1024]{1,2,0:T(8,128)(2,1)S(1)}, bf16[2,256,1024]{1,2,0:T(8,128)(2,1)}, u32[]{:S(2)}, u32[]{:S(2)}) collective-permute-start(bf16[2,256,1024]{1,2,0:T(8,128)(2,1)S(1)} %pad_maximum_fusion), channel_id=1, source_target_pairs={{0,4},{4,8},{8,12},{12,16},{16,20},{20,24},{24,28},{1,5},{5,9},{9,... | collective-permute-start | bytes 3145736 | tf_op jit(solution)/shard_map/ppermute | solution.py:16
  13.3 63.0 %collective-permute-start.1 = (bf16[2,256,1024]{1,2,0:T(8,128)(2,1)S(1)}, bf16[2,256,1024]{1,2,0:T(8,128)(2,1)}, u32[]{:S(2)}, u32[]{:S(2)}) collective-permute-start(bf16[2,256,1024]{1,2,0:T(8,128)(2,1)S(1)} %pad_maximum_fusion), channel_id=1, source_target_pairs={{0,8},{4,12},{8,16},{12,20},{16,24},{20,28},{1,9},{5,13},{9,17},{1... | collective-permute-start | bytes 3145736 | tf_op jit(solution)/shard_map/ppermute | solution.py:16
  17.7 58.5 %collective-permute-start = (bf16[2,256,1024]{1,2,0:T(8,128)(2,1)S(1)}, bf16[2,256,1024]{1,2,0:T(8,128)(2,1)}, u32[]{:S(2)}, u32[]{:S(2)}) collective-permute-start(bf16[2,256,1024]{1,2,0:T(8,128)(2,1)S(1)} %pad_maximum_fusion), channel_id=1, source_target_pairs={{0,12},{4,16},{8,20},{12,24},{16,28},{1,13},{5,17},{9,21},{13,25},... | collective-permute-start | bytes 3145736 | tf_op jit(solution)/shard_map/ppermute | solution.py:16
Sparse Core Ops, SparseCore 0:
  98.1 72.4 reduce-scatter.1
where the time goes:
time: 180 us
  waiting for transfers between devices  71.7 us (40%)
  blocking collectives  53.3 us (30%)
  matrix products  17.9 us (10%)
  between operations  14.2 us (8%)
  starting transfers between devices  12.1 us (7%)
  local copies, waits for them, and re-layouts  8.24 us (5%)
  other arithmetic  2.61 us (1%)
    reduce_scatter x1, waiting for transfers between devices, body(): lax.psum_scatter(lax.dot_general(cotangent, disc_clip, (((0,), (0,)), (()...  71.6 us
    all_gather x1, blocking collectives, body(): incoming = lax.all_gather(history, 'tm', axis=0, tiled=True)  53.3 us
    ppermute x3, starting transfers between devices, from_behind(): return lax.ppermute(x, axis, pairs)  12.1 us
    sub x1, matrix products, body(): weights = jnp.exp(scores - row_max)  7.24 us
    unnamed x13, local copies, waits for them, and re-layouts  6.14 us
    dot_general x1, matrix products, body(): lax.dot_general(cotangent, disc_clip, (((0,), (0,)), ((), ())), preferred...  5.62 us
    dot_general x1, matrix products, body(): jnp.einsum('hqk,khd->qhd', probs, value_window, preferred_element_type=jn...  4.82 us
  transfers between devices with their start and end apart: 4, of which 1 were waited for; matrix products, arithmetic and copies ran while one was open for 1% of the time, Pallas kernels for 0%

commit v1 on v0

--- a/solution.py
+++ b/solution.py
@@ -3,11 +3,14 @@
 import jax
 import jax.numpy as jnp
 from jax import lax
+from jax.experimental import pallas as pl
+from jax.experimental.pallas import tpu as pltpu
 from jax.sharding import PartitionSpec as P
 
 HD = 128
 TPF = 64
 WINB = 4
+VMEM_LIMIT = 48 * 1024 * 1024
 
 
 def from_behind(x, axis, by):
@@ -16,7 +19,7 @@
     return lax.ppermute(x, axis, pairs)
 
 
-def body(query_rows, key_rows, value_rows, frame_counts, history, offsets, cotangent):
+def window_body(query_rows, key_rows, value_rows, frame_counts, history, offsets, cotangent):
     tok_rows, feat_width = query_rows.shape
     local_heads = feat_width // HD
     block_total = lax.axis_size("tm")
@@ -70,6 +73,235 @@
     return (attended, disc_grad)
 
 
+def pack_kernel(n, off_ref, q_ref, k_ref, v_ref, hist_ref, cot_ref, out_ref):
+    own = lax.axis_index("tm")
+    tok = q_ref.shape[0]
+    tile = hist_ref.shape[0]
+    clip_rows = n * tile
+    cot_rows = cot_ref.shape[0]
+    cols = cot_ref.shape[1] // n
+    for h in range(n):
+        lanes = slice(h * HD, (h + 1) * HD)
+        out_ref[h, 0:tok, :] = q_ref[:, lanes]
+        out_ref[h, tok : 2 * tok, :] = k_ref[:, lanes]
+        out_ref[h, 2 * tok : 3 * tok, :] = v_ref[:, lanes]
+    base = 3 * tok
+    hist = hist_ref[...].astype(jnp.float32)
+    row = lax.broadcasted_iota(jnp.int32, (clip_rows, n * HD), 0)
+    placed = jnp.zeros((clip_rows, n * HD), jnp.float32)
+    for t in range(tile):
+        placed = jnp.where(row == own * tile + t, hist[t : t + 1, :], placed)
+    placed = placed.astype(jnp.bfloat16)
+    for h in range(n):
+        out_ref[h, base : base + clip_rows, :] = placed[:, h * HD : (h + 1) * HD]
+    base += clip_rows
+    r = lax.broadcasted_iota(jnp.int32, (clip_rows, clip_rows), 0)
+    c = lax.broadcasted_iota(jnp.int32, (clip_rows, clip_rows), 1)
+    select = jnp.zeros((clip_rows, clip_rows), jnp.float32)
+    for j in range(n):
+        src = lax.rem(own - off_ref[0, j] + 2 * n, n)
+        for t in range(tile):
+            select = jnp.where((c == j * tile + t) & (r == src * tile + t), 1.0, select)
+    by_row = jnp.dot(
+        select.astype(jnp.bfloat16), cot_ref[0:clip_rows, :], preferred_element_type=jnp.float32
+    ).astype(jnp.bfloat16)
+    for d in range(n):
+        for u in range(cols // HD):
+            lanes = slice(d * cols + u * HD, d * cols + (u + 1) * HD)
+            at = base + u * cot_rows
+            out_ref[d, at : at + clip_rows, :] = by_row[:, lanes]
+            out_ref[d, at + clip_rows : at + cot_rows, :] = cot_ref[clip_rows:cot_rows, lanes]
+
+
+def attend_kernel(n, tok, counts_ref, x_ref, out_ref):
+    half = n // 2
+    rate = math.log2(math.e) / math.sqrt(HD)
+    token = lax.broadcasted_iota(jnp.int32, (1, tok), 1)
+    bias = [
+        jnp.where(token < counts_ref[s] * TPF, 0.0, -jnp.inf).astype(jnp.float32) for s in range(n)
+    ]
+    for b in range(n):
+        first = max(0, b - (WINB - 1))
+        q = x_ref[b, 0:tok, :]
+        scores = [
+            lax.dot_general(
+                q,
+                x_ref[s, tok : 2 * tok, :],
+                (((1,), (1,)), ((), ())),
+                preferred_element_type=jnp.float32,
+            )
+            + bias[s]
+            for s in range(first, b + 1)
+        ]
+        top = jnp.max(scores[0], axis=1, keepdims=True)
+        for s in scores[1:]:
+            top = jnp.maximum(top, jnp.max(s, axis=1, keepdims=True))
+        weights = [jnp.exp2((s - top) * rate) for s in scores]
+        total = jnp.sum(weights[0], axis=1, keepdims=True)
+        for w in weights[1:]:
+            total = total + jnp.sum(w, axis=1, keepdims=True)
+        share = 1.0 / total
+        mixed = jnp.zeros((tok, HD), jnp.float32)
+        for s, w in zip(range(first, b + 1), weights):
+            mixed = mixed + jnp.dot(
+                (w * share).astype(jnp.bfloat16),
+                x_ref[s, 2 * tok : 3 * tok, :],
+                preferred_element_type=jnp.float32,
+            )
+        mixed = mixed.astype(jnp.bfloat16)
+        at = (b // 2) * tok
+        for c in range(half):
+            out_ref[2 * c + b % 2, at : at + tok, :] = mixed
+    clip_rows = out_ref.shape[1] - half * tok
+    hist = jnp.zeros((clip_rows, HD), jnp.float32)
+    for s in range(n):
+        hist = hist + x_ref[s, 3 * tok : 3 * tok + clip_rows, :].astype(jnp.float32)
+    hist = hist.astype(jnp.bfloat16)
+    for d in range(n):
+        out_ref[d, half * tok :, :] = hist
+
+
+def grad_rows(cot, a_ref, tok, clip_rows):
+    n = a_ref.shape[0]
+    half = len(cot)
+    rows = jnp.concatenate([a_ref[h, 0 : half * tok, :] for h in range(n)], axis=1)
+    hist = jnp.concatenate([a_ref[h, half * tok :, :] for h in range(n)], axis=1)
+    dims = (((0,), (0,)), ((), ()))
+    left = jnp.concatenate([x[clip_rows:] for x in cot], axis=0)
+    left_hist = jnp.concatenate([x[:clip_rows] for x in cot], axis=0)
+    out = lax.dot_general(left, rows, dims, preferred_element_type=jnp.float32)
+    return out + lax.dot_general(
+        left_hist, jnp.concatenate([hist] * half, axis=0), dims, preferred_element_type=jnp.float32
+    )
+
+
+def other_kernel(tok, clip_rows, cot_ref, a_ref, out_ref):
+    cot_rows = clip_rows + tok
+    units = cot_ref.shape[1] // cot_rows
+    cot = [
+        jnp.concatenate(
+            [cot_ref[c, u * cot_rows : (u + 1) * cot_rows, :] for u in range(units)], axis=1
+        )
+        for c in range(cot_ref.shape[0])
+    ]
+    out_ref[...] = grad_rows(cot, a_ref, tok, clip_rows).astype(jnp.bfloat16)
+
+
+def own_kernel(tok, clip_rows, x_ref, a_ref, att_ref, out_ref):
+    n = a_ref.shape[0]
+    own = lax.axis_index("tm")
+    chip = own // 2
+    side = lax.rem(own, 2)
+    cot_rows = clip_rows + tok
+    base = 3 * tok + clip_rows
+    units = (x_ref.shape[1] - base) // cot_rows
+    cot = [
+        jnp.concatenate(
+            [
+                x_ref[2 * c + side, base + u * cot_rows : base + (u + 1) * cot_rows, :]
+                for u in range(units)
+            ],
+            axis=1,
+        )
+        for c in range(n // 2)
+    ]
+    out_ref[...] = grad_rows(cot, a_ref, tok, clip_rows)
+    at = pl.multiple_of(chip * tok, tok)
+    for h in range(n):
+        att_ref[:, h * HD : (h + 1) * HD] = a_ref[h, pl.ds(at, tok), :]
+
+
+def head_body(query_rows, key_rows, value_rows, frame_counts, history, offsets, cotangent):
+    n = lax.axis_size("tm")
+    half = n // 2
+    tok, width = query_rows.shape
+    clip_rows = n * history.shape[0]
+    cot_rows, all_cols = cotangent.shape
+    cols = all_cols // n
+    base = 3 * tok + clip_rows
+    length = base + (cols // HD) * cot_rows
+    vmem = pl.BlockSpec(memory_space=pltpu.VMEM)
+    smem = pl.BlockSpec(memory_space=pltpu.SMEM)
+    params = pltpu.CompilerParams(vmem_limit_bytes=VMEM_LIMIT)
+    side = lax.rem(lax.axis_index("tm"), 2)
+    swap = [(i, i ^ 1) for i in range(n)]
+
+    packed = pl.pallas_call(
+        lambda *refs: pack_kernel(n, *refs),
+        out_shape=jax.ShapeDtypeStruct((n, length, HD), jnp.bfloat16),
+        in_specs=[smem] + [vmem] * 5,
+        out_specs=vmem,
+        compiler_params=params,
+        name="pack",
+    )(offsets, query_rows, key_rows, value_rows, history, cotangent)
+    by_head = lax.all_to_all(packed, "tm", 0, 0)
+
+    for_other = lax.dynamic_slice(
+        by_head.reshape(half, 2, length, HD), (0, 1 - side, base, 0), (half, 1, length - base, HD)
+    ).reshape(half, length - base, HD)
+    from_other = lax.ppermute(for_other, "tm", swap)
+
+    spread = pl.pallas_call(
+        lambda *refs: attend_kernel(n, tok, *refs),
+        out_shape=jax.ShapeDtypeStruct((n, half * tok + clip_rows, HD), jnp.bfloat16),
+        in_specs=[smem, vmem],
+        out_specs=vmem,
+        compiler_params=params,
+        cost_estimate=pl.CostEstimate(
+            flops=4 * n * tok * WINB * tok * HD,
+            bytes_accessed=2 * 2 * n * length * HD,
+            transcendentals=n * tok * WINB * tok,
+        ),
+        name="attend",
+    )(frame_counts, by_head)
+    gathered = lax.all_to_all(spread, "tm", 0, 0)
+
+    grad_cost = pl.CostEstimate(
+        flops=2 * cols * half * cot_rows * width,
+        bytes_accessed=2 * n * (half * tok + clip_rows) * HD + 4 * cols * width,
+        transcendentals=0,
+    )
+    other = pl.pallas_call(
+        lambda *refs: other_kernel(tok, clip_rows, *refs),
+        out_shape=jax.ShapeDtypeStruct((cols, width), jnp.bfloat16),
+        in_specs=[vmem, vmem],
+        out_specs=vmem,
+        compiler_params=params,
+        cost_estimate=grad_cost,
+        name="grad_other",
+    )(from_other, gathered)
+    arrived = lax.ppermute(other, "tm", swap)
+    attended, own = pl.pallas_call(
+        lambda *refs: own_kernel(tok, clip_rows, *refs),
+        out_shape=(
+            jax.ShapeDtypeStruct((tok, width), jnp.bfloat16),
+            jax.ShapeDtypeStruct((cols, width), jnp.float32),
+        ),
+        in_specs=[vmem, vmem],
+        out_specs=(vmem, vmem),
+        compiler_params=params,
+        cost_estimate=grad_cost,
+        name="grad_own",
+    )(by_head, gathered)
+    return attended, own + arrived.astype(jnp.float32)
+
+
+def body(query_rows, key_rows, value_rows, frame_counts, history, offsets, cotangent):
+    n = lax.axis_size("tm")
+    tok, width = query_rows.shape
+    by_heads = (
+        n % 2 == 0
+        and width == n * HD
+        and offsets.shape[1] == n
+        and cotangent.shape[0] == tok + n * history.shape[0]
+        and cotangent.shape[1] % (n * HD) == 0
+        and tok % 16 == 0
+        and (n * history.shape[0]) % 16 == 0
+    )
+    plan = head_body if by_heads else window_body
+    return plan(query_rows, key_rows, value_rows, frame_counts, history, offsets, cotangent)
+
+
 def solution(mesh):
     in_specs = (
         P("tm", "head"),

time: 180 us -> 90.9 us (0.51)
  waiting for transfers between devices: 71.7 us -> 26.5 us
  matrix products: 17.9 us -> 0 us
  blocking collectives: 53.3 us -> 38.2 us
  between operations: 14.2 us -> 0.72 us
  Pallas kernels: 0 us -> 11.8 us
  starting transfers between devices: 12.1 us -> 4.85 us
    reduce_scatter x1 -> x0, waiting for transfers between devices: 71.6 us -> none  [body(): lax.psum_scatter(lax.dot_general(cotangent, disc_clip, (((0,), (0,)), (()...]
    all_gather x1 -> x0, blocking collectives: 53.3 us -> none  [body(): incoming = lax.all_gather(history, 'tm', axis=0, tiled=True)]
    all_to_all x0 -> x1, blocking collectives: none -> 38.2 us  [head_body(): by_head = lax.all_to_all(packed, 'tm', 0, 0)]
    all_to_all x0 -> x1, waiting for transfers between devices: none -> 24.8 us  [head_body(): gathered = lax.all_to_all(spread, 'tm', 0, 0)]
    pallas_call x0 -> x4, Pallas kernels: none -> 11.8 us  [the longest x1 5.04 us: head_body(): pl.pallas_call(lambda *refs: attend_kernel(n, tok, *refs), out_shape=jax....]
    ppermute x3 -> x2, starting transfers between devices: 12.1 us -> 0.5 us  [the longest x1 0.43 us: head_body(): from_other = lax.ppermute(for_other, 'tm', swap)]
    dot_general x3 -> x0, matrix products: 10.6 us -> none  [the longest x1 5.62 us: body(): lax.dot_general(cotangent, disc_clip, (((0,), (0,)), ((), ())), preferred...]
    sub x1 -> x0, matrix products: 7.24 us -> none  [body(): weights = jnp.exp(scores - row_max)]
  transfers between devices with their start and end apart: 4 -> 3, of which waited for: 1 -> 2; matrix products, arithmetic and copies ran while one was open for 1% -> 0% of each run, Pallas kernels for 0% -> 4%
where the time goes in v1:
time: 90.9 us; the launch traced here: 90.4 us
  blocking collectives  38.2 us (42%)
  waiting for transfers between devices  26.5 us (29%)
  Pallas kernels  11.8 us (13%)
  local copies, waits for them, and re-layouts  7.09 us (8%)
  starting transfers between devices  4.85 us (5%)
  other arithmetic  1.16 us (1%)
    all_to_all x1, blocking collectives, head_body(): by_head = lax.all_to_all(packed, 'tm', 0, 0)  38.2 us
    all_to_all x1, waiting for transfers between devices, head_body(): gathered = lax.all_to_all(spread, 'tm', 0, 0)  24.8 us
    unnamed x16, local copies, waits for them, and re-layouts  7.04 us
    pallas_call x1, Pallas kernels, head_body(): pl.pallas_call(lambda *refs: attend_kernel(n, tok, *refs), out_shape=jax....  5.04 us
    all_to_all x1, starting transfers between devices, head_body(): gathered = lax.all_to_all(spread, 'tm', 0, 0)  4.35 us
    pallas_call x1, Pallas kernels, head_body(): pl.pallas_call(lambda *refs: own_kernel(tok, clip_rows, *refs), out_shape...  3.25 us
    pallas_call x1, Pallas kernels, head_body(): pl.pallas_call(lambda *refs: other_kernel(tok, clip_rows, *refs), out_sha...  2.46 us
  transfers between devices with their start and end apart: 3, of which 2 were waited for; matrix products, arithmetic and copies ran while one was open for 0% of the time, Pallas kernels for 4%

profile of v1, /device:TPU:0, one launch (start us, length us, event | category | flops | bytes accessed | tf_op | source)
XLA Modules:
  0.0 90.4 jit_solution(10829079169174833011)
XLA Ops:
  0.6 0.0 copy-start.1
  0.6 1.2 %copy-done.1 = bf16[272,2048]{1,0:T(8,128)(2,1)S(1)} copy-done((bf16[272,2048]{1,0:T(8,128)(2,1)S(1)}, bf16[272,2048]{1,0:T(8,128)(2,1)}, u32[]{:S(2)}) %copy-start.1) | copy-done | bytes 1114136
  1.9 0.0 copy-start.2
  1.9 1.0 %copy-done.2 = bf16[256,1024]{1,0:T(8,128)(2,1)S(1)} copy-done((bf16[256,1024]{1,0:T(8,128)(2,1)S(1)}, bf16[256,1024]{1,0:T(8,128)(2,1)}, u32[]{:S(2)}) %copy-start.2) | copy-done | bytes 524312
  2.9 0.0 copy-start.3
  2.9 1.0 %copy-done.3 = bf16[256,1024]{1,0:T(8,128)(2,1)S(1)} copy-done((bf16[256,1024]{1,0:T(8,128)(2,1)S(1)}, bf16[256,1024]{1,0:T(8,128)(2,1)}, u32[]{:S(2)}) %copy-start.3) | copy-done | bytes 524312
  4.0 0.0 copy-start.4
  4.0 1.0 %copy-done.4 = bf16[256,1024]{1,0:T(8,128)(2,1)S(1)} copy-done((bf16[256,1024]{1,0:T(8,128)(2,1)S(1)}, bf16[256,1024]{1,0:T(8,128)(2,1)}, u32[]{:S(2)}) %copy-start.4) | copy-done | bytes 524312
  5.0 0.0 copy-start.5
  5.0 0.7 copy-done.5
  5.7 0.0 copy-start.6
  5.7 0.7 copy-done.6
  6.3 1.0 %pack.1 = bf16[8,1328,128]{2,1,0:T(8,128)(2,1)S(1)} custom-call(s32[1,8]{1,0:T(1,128)S(1)} %copy-done.6, bf16[256,1024]{1,0:T(8,128)(2,1)S(1)} %copy-done.2, bf16[256,1024]{1,0:T(8,128)(2,1)S(1)} %copy-done.3, bf16[256,1024]{1,0:T(8,128)(2,1)S(1)} %copy-done.4, bf16[2,1024]{1,0:T(2,128)(2,1)S(1)} %copy-done.5, bf16[272,2048]{1,0:T(8,128)(2,1)S(1)} %copy-done.1), custom_call_target="tpu_custom_call" | custom-call | tf_op jit(solution)/shard_map/pack/pallas_call | solution.py:229
  7.4 0.0 copy-start.7
  7.4 38.2 %all_to_all.10.refs_1_.refs_0_ = bf16[8,1328,128]{2,1,0:T(8,128)(2,1)S(1)} all-to-all(bf16[8,1328,128]{2,1,0:T(8,128)(2,1)S(1)} %pack.1), channel_id=1, replica_groups=mesh['tm'=8,'head'=4] {'tm'}, dimensions={0} | all-to-all | bytes 5439488 | tf_op jit(solution)/shard_map/all_to_all | solution.py:237
  45.7 0.0 copy-done.7
  45.7 5.0 %attend.1 = bf16[8,1040,128]{2,1,0:T(8,128)(2,1)S(1)} custom-call(s32[8]{0:T(128)S(1)} %copy-done.7, bf16[8,1328,128]{2,1,0:T(8,128)(2,1)S(1)} %all_to_all.10.refs_1_.refs_0_), custom_call_target="tpu_custom_call" | custom-call | flops 1073741824 | bytes 5439488 | tf_op jit(solution)/shard_map/attend/pallas_call | solution.py:244
  50.7 0.0 copy-start
  50.7 1.3 %copy-done = bf16[8,1040,128]{2,1,0:T(8,128)(2,1)} copy-done((bf16[8,1040,128]{2,1,0:T(8,128)(2,1)}, bf16[8,1040,128]{2,1,0:T(8,128)(2,1)S(1)}, u32[]{:S(2)}) %copy-start) | copy-done | bytes 2129944
  52.0 4.4 %all-to-all-start.1 = ((bf16[8,1040,128]{2,1,0:T(8,128)(2,1)}), bf16[8,1040,128]{2,1,0:T(8,128)(2,1)}, u32[]{:S(2)}, u32[]{:S(2)}) async-start(bf16[8,1040,128]{2,1,0:T(8,128)(2,1)} %copy-done), calls=%async_computation.1 | async-start | bytes 4259840 | tf_op jit(solution)/shard_map/all_to_all | solution.py:257
  56.5 0.4 collective-permute-start
  56.9 1.7 %collective-permute-done.refs_0_ = bf16[4,544,128]{2,1,0:T(8,128)(2,1)S(1)} collective-permute-done((bf16[4,544,128]{2,1,0:T(8,128)(2,1)S(1)}, bf16[4,544,128]{2,1,0:T(8,128)(2,1)S(1)}, u32[]{:S(2)}, u32[]{:S(2)}) %collective-permute-start) | collective-permute-done | bytes 557088 | tf_op jit(solution)/shard_map/ppermute | solution.py:242
  58.6 24.8 %all-to-all-done.1.refs_1_ = bf16[8,1040,128]{2,1,0:T(8,128)(2,1)} async-done(((bf16[8,1040,128]{2,1,0:T(8,128)(2,1)}), bf16[8,1040,128]{2,1,0:T(8,128)(2,1)}, u32[]{:S(2)}, u32[]{:S(2)}) %all-to-all-start.1) | async-done | bytes 2129952 | tf_op jit(solution)/shard_map/all_to_all | solution.py:257
  83.4 2.5 %grad_other.1 = bf16[256,1024]{1,0:T(8,128)(2,1)S(1)} custom-call(bf16[4,544,128]{2,1,0:T(8,128)(2,1)S(1)} %collective-permute-done.refs_0_, bf16[8,1040,128]{2,1,0:T(8,128)(2,1)} %all-to-all-done.1.refs_1_), custom_call_target="tpu_custom_call" | custom-call | flops 570425344 | bytes 3178496 | tf_op jit(solution)/shard_map/grad_other/pallas_call | solution.py:264
  85.9 0.1 collective-permute-start.1
  85.9 3.2 %grad_own.1 = (bf16[256,1024]{1,0:T(8,128)(2,1)}, f32[256,1024]{1,0:T(8,128)S(1)}) custom-call(bf16[8,1328,128]{2,1,0:T(8,128)(2,1)S(1)} %all_to_all.10.refs_1_.refs_0_, bf16[8,1040,128]{2,1,0:T(8,128)(2,1)} %all-to-all-done.1.refs_1_), custom_call_target="tpu_custom_call" | custom-call | flops 570425344 | bytes 3178496 | tf_op jit(solution)/shard_map/grad_own/pallas_call | solution.py:274
  89.2 0.0 collective-permute-done.1
  89.2 1.2 %convert_add_fusion = f32[256,1024]{1,0:T(8,128)} fusion(f32[256,1024]{1,0:T(8,128)S(1)} %get-tuple-element.5, bf16[256,1024]{1,0:T(8,128)(2,1)S(1)} %collective-permute-done.1), kind=kLoop, calls=%fused_computation | loop fusion | flops 524288 | bytes 2621440 | tf_op jit(solution)/shard_map/add | solution.py:286
  (1 shorter events, 0.0 us)
Async XLA Ops:
  0.6 1.2 %copy-start.1 = (bf16[272,2048]{1,0:T(8,128)(2,1)S(1)}, bf16[272,2048]{1,0:T(8,128)(2,1)}, u32[]{:S(2)}) copy-start(bf16[272,2048]{1,0:T(8,128)(2,1)} %refs_5_.1) | copy-start | bytes 3342340
  1.9 1.0 %copy-start.2 = (bf16[256,1024]{1,0:T(8,128)(2,1)S(1)}, bf16[256,1024]{1,0:T(8,128)(2,1)}, u32[]{:S(2)}) copy-start(bf16[256,1024]{1,0:T(8,128)(2,1)} %refs_1_.1) | copy-start | bytes 1572868
  2.9 1.0 %copy-start.3 = (bf16[256,1024]{1,0:T(8,128)(2,1)S(1)}, bf16[256,1024]{1,0:T(8,128)(2,1)}, u32[]{:S(2)}) copy-start(bf16[256,1024]{1,0:T(8,128)(2,1)} %refs_2_.1) | copy-start | bytes 1572868
  4.0 1.0 %copy-start.4 = (bf16[256,1024]{1,0:T(8,128)(2,1)S(1)}, bf16[256,1024]{1,0:T(8,128)(2,1)}, u32[]{:S(2)}) copy-start(bf16[256,1024]{1,0:T(8,128)(2,1)} %refs_3_.1) | copy-start | bytes 1572868
  5.0 0.7 copy-start.5
  5.7 0.7 copy-start.6
  7.4 38.3 %copy-start.7 = (s32[8]{0:T(128)S(1)}, s32[8]{0:T(128)}, u32[]{:S(2)}) copy-start(s32[8]{0:T(128)} %refs_0_.3) | copy-start | bytes 100
  50.7 1.3 %copy-start = (bf16[8,1040,128]{2,1,0:T(8,128)(2,1)}, bf16[8,1040,128]{2,1,0:T(8,128)(2,1)S(1)}, u32[]{:S(2)}) copy-start(bf16[8,1040,128]{2,1,0:T(8,128)(2,1)S(1)} %attend.1) | copy-start | bytes 6389764
  52.0 31.4 %all-to-all-start.1 = ((bf16[8,1040,128]{2,1,0:T(8,128)(2,1)}), bf16[8,1040,128]{2,1,0:T(8,128)(2,1)}, u32[]{:S(2)}, u32[]{:S(2)}) async-start(bf16[8,1040,128]{2,1,0:T(8,128)(2,1)} %copy-done), calls=%async_computation.1 | async-start | bytes 4259840 | tf_op jit(solution)/shard_map/all_to_all | solution.py:257
  56.5 2.1 %collective-permute-start = (bf16[4,544,128]{2,1,0:T(8,128)(2,1)S(1)}, bf16[4,544,128]{2,1,0:T(8,128)(2,1)S(1)}, u32[]{:S(2)}, u32[]{:S(2)}) collective-permute-start(bf16[4,544,128]{2,1,0:T(8,128)(2,1)S(1)} %dynamic-slice_bitcast_fusion), channel_id=1, source_target_pairs={{0,4},{4,0},{8,12},{12,8},{16,20},{20,16},{24,28},{28,24},{1,5},{5... | collective-permute-start | bytes 1671176 | tf_op jit(solution)/shard_map/ppermute | solution.py:242
  85.9 3.3 %collective-permute-start.1 = (bf16[256,1024]{1,0:T(8,128)(2,1)S(1)}, bf16[256,1024]{1,0:T(8,128)(2,1)S(1)}, u32[]{:S(2)}, u32[]{:S(2)}) collective-permute-start(bf16[256,1024]{1,0:T(8,128)(2,1)S(1)} %grad_other.1), channel_id=1, source_target_pairs={{0,4},{4,0},{8,12},{12,8},{16,20},{20,16},{24,28},{28,24},{1,5},{5... | collective-permute-start | bytes 1572872 | tf_op jit(solution)/shard_map/ppermute | solution.py:273
